TPU v7x, 512 devices: a whole 4x8x8 slice. The times are simulated.
512 devices in a mesh: dp: 32 (over z, x), mem: 16 (over y, core).
Axes of the slice: x: 4, y: 8, z: 8, core: 2. Of those that a mesh axis runs over, the one named last changes fastest.
Arguments:
- table: bfloat16 [2048, 4096], P(None, 'mem'), may hold values from -6 to 6
- block_ids: int32 [512, 4], P('dp'), may hold values from 0 to 15, all different within a row
- weights: bfloat16 [65536, 512], P(('dp', 'mem')), may hold values from -0.25 to 0.25
- grad_out: bfloat16 [65536, 4096], P(('dp', 'mem')), may hold values from -0.1796875 to 0.1796875
Outputs:
- values_out: bfloat16 [65536, 4096], P(('dp', 'mem'))
- grad_weights: bfloat16 [65536, 512], P(('dp', 'mem'))
- grad_table: bfloat16 [2048, 4096], P(None, 'mem')
Inputs may be any that keep to these rules, and one draw needn't show every extreme that they name: `block_ids`: the 4 block ids of one tile are distinct.
All inputs are finite; a program needn't handle non-finite values.
Results may differ from a plain program's by a relative error of at most 0.001.
Values may be sent and summed in bfloat16 or wider, within the bound.
A program may use at most 64 MiB of HBM per device.

v0:
```python
import jax
import jax.numpy as jnp
from jax import lax
from jax.sharding import PartitionSpec as P

BLOCK = 128
SEL = 4
TILE = 128
BLOCKS = 16


def shards(table, block_ids, weights, grad_out):
    tok_dev = weights.shape[0]
    width = table.shape[1]
    n_tiles = block_ids.shape[0]
    group = n_tiles * TILE
    blocks = table.reshape(BLOCKS, BLOCK, width)
    chosen = blocks[block_ids].reshape(n_tiles, SEL * BLOCK, width)
    all_weights = lax.all_gather(weights, "mem", axis=0, tiled=True)
    tile_w = all_weights.reshape(n_tiles, TILE, SEL * BLOCK)
    out_part = jnp.einsum("tqk,tkc->tqc", tile_w, chosen, preferred_element_type=jnp.float32)
    out_part = out_part.astype(jnp.bfloat16).reshape(group, width)
    values_out = lax.all_to_all(out_part, "mem", split_axis=0, concat_axis=1, tiled=True)
    grad_part = lax.all_to_all(grad_out, "mem", split_axis=1, concat_axis=0, tiled=True)
    tile_g = grad_part.reshape(n_tiles, TILE, width)
    term = jnp.einsum("tqc,tkc->tqk", tile_g, chosen, preferred_element_type=jnp.float32)
    grad_weights = lax.psum_scatter(
        term.reshape(lax.axis_size("mem") * tok_dev, SEL * BLOCK),
        "mem",
        scatter_dimension=0,
        tiled=True,
    ).astype(jnp.bfloat16)
    dsel = jnp.einsum("tqk,tqc->tkc", tile_w, tile_g, preferred_element_type=jnp.float32)
    dsel = dsel.reshape(n_tiles * SEL, BLOCK * width)
    onehot = (
        block_ids.reshape(n_tiles * SEL, 1) == jnp.arange(BLOCKS, dtype=jnp.int32)[None, :]
    ).astype(jnp.float32)
    table_term = jnp.dot(
        onehot.T, dsel, precision=lax.Precision.HIGHEST, preferred_element_type=jnp.float32
    )
    table_term = table_term.reshape(BLOCKS * BLOCK, width)
    grad_table = lax.psum(table_term, "dp").astype(jnp.bfloat16)
    return (values_out, grad_weights, grad_table)


def solution(mesh):
    return jax.shard_map(
        shards,
        mesh=mesh,
        in_specs=(P(None, "mem"), P("dp", None), P(("dp", "mem"), None), P(("dp", "mem"), None)),
        out_specs=(P(("dp", "mem"), None), P(("dp", "mem"), None), P(None, "mem")),
        check_vma=False,
    )
```

profile of v0, /device:TPU:8, one launch (start us, length us, event | category | flops | bytes accessed | tf_op | source)
XLA Modules:
  0.0 282.2 jit_solution(12269953814721474803)
XLA Ops:
  7.2 0.0 copy-start
  7.2 0.0 copy-start.1
  7.2 0.0 all-gather.2.cloned.1.call-start
  7.2 0.7 all-gather.2.cloned.1.call-update
  7.9 1.6 copy.14
  9.5 1.3 copy.15
  10.9 9.3 %all-to-all-start.1 = ((bf16[128,16,256]{2,0,1:T(8,128)(2,1)}), bf16[128,16,256]{2,0,1:T(8,128)(2,1)S(1)}, u32[]{:S(2)}, u32[]{:S(2)}) async-start(bf16[128,16,256]{2,0,1:T(8,128)(2,1)} %copy.15), calls=%async_computation.1 | async-start | bytes 2097152 | tf_op jit(solution)/shard_map/all_to_all | solution.py:24
  20.1 0.0 reduce-scatter.2.cloned.1.call-start
  20.2 0.0 copy-done.1
  20.2 0.1 copy.12
  20.3 0.1 reshape.44
  20.4 0.0 copy-done
  20.4 2.8 gather_fusion
  23.2 26.5 %all-to-all-done.1 = bf16[128,16,256]{2,0,1:T(8,128)(2,1)S(1)} async-done(((bf16[128,16,256]{2,0,1:T(8,128)(2,1)}), bf16[128,16,256]{2,0,1:T(8,128)(2,1)S(1)}, u32[]{:S(2)}, u32[]{:S(2)}) %all-to-all-start.1) | async-done | bytes 1048608 | tf_op jit(solution)/shard_map/all_to_all | solution.py:24
  49.6 5.7 %fusion.3 = f32[16,512,128]{1,2,0:T(8,128)} fusion(bf16[16,512,256]{2,1,0:T(8,128)(2,1)} %bitcast.23, bf16[128,16,256]{2,0,1:T(8,128)(2,1)S(1)} %all-to-all-done.1), kind=kOutput, calls=%fused_computation.5 | convolution fusion | flops 536870912 | bytes 9437184 | tf_op jit(solution)/shard_map/tqc,tkc->tqk/dot_general | solution.py:26
  55.3 0.0 reduce-scatter.2.cloned.1.call-update
  55.3 0.1 copy.16
  55.4 0.1 eq.15
  55.5 8.3 %all-gather.2.cloned.1.call-done = bf16[2048,512]{1,0:T(8,128)(2,1)} async-done(((bf16[128,512]{1,0:T(8,128)(2,1)}), bf16[2048,512]{1,0:T(8,128)(2,1)}) %all-gather.2.cloned.1.call-update) | async-done | bytes 2097168 | tf_op jit(solution)/shard_map/all_gather | solution.py:19
  63.8 5.2 %fusion = bf16[16,128,256]{1,2,0:T(8,128)(2,1)} fusion(bf16[16,512,256]{2,1,0:T(8,128)(2,1)} %bitcast.24, bf16[16,128,512]{2,1,0:T(8,128)(2,1)} %bitcast.26), kind=kOutput, calls=%fused_computation.2 | convolution fusion | flops 537395200 | bytes 7340032 | tf_op jit(solution)/shard_map/tqk,tkc->tqc/dot_general | solution.py:21
  69.0 5.2 %all-to-all-start = ((bf16[16,128,256]{1,2,0:T(8,128)(2,1)}), bf16[16,128,256]{1,2,0:T(8,128)(2,1)S(1)}, u32[]{:S(2)}, u32[]{:S(2)}) async-start(bf16[16,128,256]{1,2,0:T(8,128)(2,1)} %fusion), calls=%async_computation | async-start | bytes 2097152 | tf_op jit(solution)/shard_map/all_to_all | solution.py:23
  74.2 6.1 %fusion.1 = f32[16,512,256]{2,1,0:T(8,128)} fusion(bf16[16,128,512]{2,1,0:T(8,128)(2,1)} %bitcast.27, bf16[128,16,256]{2,0,1:T(8,128)(2,1)S(1)} %all-to-all-done.1), kind=kOutput, calls=%fused_computation.3 | convolution fusion | flops 536870912 | bytes 11534336 | tf_op jit(solution)/shard_map/tqk,tqc->tkc/dot_general | solution.py:33
  80.3 9.5 %reshape.40 = f32[64,32768]{1,0:T(8,128)} reshape(f32[16,512,256]{2,1,0:T(8,128)} %fusion.1) | data formatting | bytes 16777216 | tf_op jit(solution)/shard_map/reshape | solution.py:34
  89.8 7.7 %fusion.5 = f32[16,32768]{1,0:T(8,128)} fusion(f32[64,32768]{1,0:T(8,128)} %reshape.40, s32[64]{0:T(128)S(1)} %eq.15), kind=kOutput, calls=%fused_computation.8 | convolution fusion | flops 402654208 | bytes 10486016 | tf_op jit(solution)/shard_map/dot_general | solution.py:38
  97.5 2.7 reshape.41
  100.2 172.2 %all-reduce.1 = bf16[2048,256]{1,0:T(8,128)(2,1)} all-reduce(f32[2048,256]{1,0:T(8,128)} %reshape.41), channel_id=1, replica_groups=mesh['dp'=32,'mem'=16] {'dp'}, use_global_device_ids=true, to_apply=%region_1.0 | all-reduce | flops 524288 | bytes 3145728 | tf_op jit(solution)/shard_map/psum | solution.py:42
  272.4 0.0 all-to-all-done
  272.4 1.3 copy.18
  273.7 0.0 reduce-scatter.2.cloned.1.call-done
  273.7 1.6 convert_element_type.15
  (2 shorter events, 0.0 us)
Async XLA Ops:
  7.2 13.2 %copy-start = (bf16[2048,256]{1,0:T(8,128)(2,1)S(1)}, bf16[2048,256]{1,0:T(8,128)(2,1)}, u32[]{:S(2)}) copy-start(bf16[2048,256]{1,0:T(8,128)(2,1)} %param.4) | copy-start | bytes 3145732
  7.2 13.0 %copy-start.1 = (s32[16,4]{0,1:T(4,128)S(1)}, s32[16,4]{0,1:T(4,128)}, u32[]{:S(2)}) copy-start(s32[16,4]{0,1:T(4,128)} %param.5) | copy-start | bytes 772
  7.2 56.6 %all-gather.2.cloned.1.call-start = ((), (), s32[]{:S(2)}) async-start(), calls=%async_computation.3 | async-start | bytes 2228224 | tf_op jit(solution)/shard_map/all_gather | solution.py:19
  10.9 38.8 %all-to-all-start.1 = ((bf16[128,16,256]{2,0,1:T(8,128)(2,1)}), bf16[128,16,256]{2,0,1:T(8,128)(2,1)S(1)}, u32[]{:S(2)}, u32[]{:S(2)}) async-start(bf16[128,16,256]{2,0,1:T(8,128)(2,1)} %copy.15), calls=%async_computation.1 | async-start | bytes 2097152 | tf_op jit(solution)/shard_map/all_to_all | solution.py:24
  20.1 253.6 %reduce-scatter.2.cloned.1.call-start = ((), (), s32[]{:S(2)}) async-start(), calls=%async_computation.4 | async-start | bytes 4456448 | tf_op jit(solution)/shard_map/reduce_scatter | solution.py:27
  69.0 203.4 %all-to-all-start = ((bf16[16,128,256]{1,2,0:T(8,128)(2,1)}), bf16[16,128,256]{1,2,0:T(8,128)(2,1)S(1)}, u32[]{:S(2)}, u32[]{:S(2)}) async-start(bf16[16,128,256]{1,2,0:T(8,128)(2,1)} %fusion), calls=%async_computation | async-start | bytes 2097152 | tf_op jit(solution)/shard_map/all_to_all | solution.py:23
Sparse Core Ops, SparseCore 0:
  10.1 53.6 all-gather.1
  66.6 74.5 reduce-scatter.1
where the time goes:
time: 283 us; the launch traced here: 282 us
  blocking collectives  172 us (61%)
  waiting for transfers between devices  35.5 us (13%)
  matrix products  24.6 us (9%)
  local copies, waits for them, and re-layouts  19.6 us (7%)
  starting transfers between devices  14.5 us (5%)
  between operations  14.1 us (5%)
    psum x1, blocking collectives, shards(): grad_table = lax.psum(table_term, 'dp').astype(jnp.bfloat16)  172 us
    all_to_all x1, waiting for transfers between devices, shards(): lax.all_to_all(grad_out, 'mem', split_axis=1, concat_axis=0, tiled=True)  26.5 us
    reshape x1, local copies, waits for them, and re-layouts, shards(): dsel = dsel.reshape(n_tiles * SEL, BLOCK * width)  9.51 us
    all_to_all x1, starting transfers between devices, shards(): lax.all_to_all(grad_out, 'mem', split_axis=1, concat_axis=0, tiled=True)  9.27 us
    all_gather x1, waiting for transfers between devices, shards(): all_weights = lax.all_gather(weights, 'mem', axis=0, tiled=True)  8.29 us
    dot_general x1, matrix products, shards(): jnp.dot(onehot.T, dsel, precision=lax.Precision.HIGHEST, preferred_elemen...  7.66 us
    dot_general x1, matrix products, shards(): jnp.einsum('tqk,tqc->tkc', tile_w, tile_g, preferred_element_type=jnp.flo...  6.11 us
  transfers between devices with their start and end apart: 4, of which 2 were waited for; matrix products, arithmetic and copies ran while one was open for 16% of the time, Pallas kernels for 0%

commit v1 on v0

v1 whole, which is shorter than its diff:
```python
import functools

import jax
import jax.numpy as jnp
from jax import lax
from jax.experimental import pallas as pl
from jax.experimental.pallas import tpu as pltpu
from jax.sharding import PartitionSpec as P

MESH = pl.DeviceIdType.MESH
BLOCK = 128
SEL = 4
TILE = 128
HALF = 128
NX = 4


def kernel(
    nx, ny, nz, rows, width,
    ids_ref, idx_ref, table_ref, w_ref, g_ref,
    vout_ref, gw_ref, tout_ref,
    T, Wt, Gr, acc, ra, rb, r2a, r2b, O, V, GW,
    send, recv, local,
):
    dp, mem = lax.axis_index("dp"), lax.axis_index("mem")
    z, x = dp // nx, dp % nx
    y, c = mem // 2, mem % 2
    s = 1 - 2 * c
    n_mem = 2 * ny
    blocks = rows // BLOCK
    zero_slot = n_mem * SEL
    na = (ny - 1) // 2
    nb = ny - 1 - na
    xr, zr, sh = rows // nx, rows // nz, rows // (nx * nz)

    def dev(xx, yy, zz, cc):
        return (zz * nx + xx, yy * 2 + cc)

    sib = dev(x, y, z, 1 - c)

    def wrap(v, n):
        return (v + 4 * n) % n

    def row(start, size):
        return pl.ds(pl.multiple_of(start, size), size)

    def rows_of(ref, lead, start, size):
        if size >= BLOCK:
            return ref.at[(*lead, pl.ds(start // BLOCK, size // BLOCK))]
        return ref.at[(*lead, start // BLOCK, row(start % BLOCK, size))]

    everything = []

    def remote(src, dst, device):
        k = len(everything)
        copy = pltpu.make_async_remote_copy(
            src_ref=src, dst_ref=dst, send_sem=send.at[k], recv_sem=recv.at[k],
            device_id=device, device_id_type=MESH,
        )
        copy.start()
        everything.append(copy)
        return copy

    def next_x(d):
        return dev(wrap(x + d, nx), y, z, c)

    def next_y(d):
        return dev(x, wrap(y + d, ny), z, c)

    def next_z(d):
        return dev(x, y, wrap(z + d, nz), c)

    barrier = pltpu.get_barrier_semaphore()
    peers = [(dp, (mem + k) % n_mem) for k in range(1, n_mem)]
    peers += [next_x(k) for k in range(1, nx)] + [next_z(k) for k in range(1, nz)]
    for p in peers:
        pl.semaphore_signal(barrier, inc=1, device_id=p, device_id_type=MESH)
    pl.semaphore_wait(barrier, len(peers))

    share_a, share_b = z * zr + x * sh, x * xr + z * sh
    order = sorted(range(1, ny), key=lambda j: min(j, ny - j))
    shares = {}
    for j in order:
        at = share_a if j <= na else share_b
        shares[j] = remote(rows_of(table_ref, (), at, sh), rows_of(T, (j, c), at, sh), next_y(-j))
    own = pltpu.make_async_copy(table_ref, T.at[0, c], local.at[0])
    own.start()

    Wt[zero_slot] = jnp.zeros((BLOCK, TILE), jnp.bfloat16)
    for k in range(SEL):
        Wt[mem * SEL + k] = w_ref[:, k * BLOCK:(k + 1) * BLOCK].astype(jnp.float32).T.astype(jnp.bfloat16)

    def w_piece(d, back):
        return Wt.at[pl.ds((wrap(y - d * back, ny) * 2 + c) * SEL, SEL)]

    def w_hop(d, h):
        p = w_piece(d, h - 1)
        return remote(p, p, next_y(d))

    sib_w = []

    def w_sib(d, back):
        p = w_piece(d, back)
        sib_w.append(remote(p, p, sib))

    wl, ws = w_hop(s, 1), (w_hop(-s, 1) if ny > 2 else None)
    w_sib(s, 0)
    sib_t = [remote(table_ref, T.at[0, c], sib)]

    g_copies = []

    def g_send(ks):
        for k in ks:
            m = (mem + k) % n_mem
            g_copies.append(
                remote(g_ref.at[:, row(m * width, width)], Gr.at[mem], (dp, m))
            )

    g_order = list(range(1, n_mem))
    per = -(-len(g_order) // (ny // 2))
    g_batches = [g_order[i:i + per] for i in range(0, len(g_order), per)]
    g_own = pltpu.make_async_copy(g_ref.at[:, row(mem * width, width)], Gr.at[mem], local.at[1])
    g_own.start()

    def ax_hop(d, h):
        p = rows_of(T, (slice(1, 1 + na), c), z * zr + wrap(x - d * (h - 1), nx) * sh, sh)
        return remote(p, p, next_x(d))

    def az_piece(d, back):
        return rows_of(T, (slice(1, 1 + na), c), wrap(z - d * back, nz) * zr, zr)

    def az_hop(d, h):
        p = az_piece(d, h - 1)
        return remote(p, p, next_z(d))

    def bz_hop(d, h):
        p = rows_of(T, (slice(1 + na, ny), c), x * xr + wrap(z - d * (h - 1), nz) * sh, sh)
        return remote(p, p, next_z(d))

    def bx_piece(d, back):
        return rows_of(T, (slice(1 + na, ny), c), wrap(x - d * back, nx) * xr, xr)

    def bx_hop(d, h):
        p = bx_piece(d, h - 1)
        return remote(p, p, next_x(d))

    def t_sib(p):
        sib_t.append(remote(p, p, sib))

    lx, lz, ly = nx // 2, nz // 2, ny // 2

    for j in range(1, ny):
        if j <= na:
            shares[j].wait_recv()
    axl = ax_hop(s, 1)
    axs = ax_hop(-s, 1) if lx > 1 else None
    for j in range(1, ny):
        if j > na:
            shares[j].wait_recv()
    bzl = bz_hop(s, 1)
    bzs = bz_hop(-s, 1) if lz > 1 else None

    azl = azs = None
    for h in range(1, max(ly, lz, lx) + 1):
        if h <= len(g_batches):
            g_send(g_batches[h - 1])
        if h <= lx:
            axl.wait_recv()
            if h < lx:
                axl = ax_hop(s, h + 1)
            if h < lx:
                axs.wait_recv()
                if h < lx - 1:
                    axs = ax_hop(-s, h + 1)
            if h == lx:
                azl = az_hop(s, 1)
                azs = az_hop(-s, 1) if lz > 1 else None
                t_sib(az_piece(s, 0))
        if h <= lz:
            bzl.wait_recv()
            if h < lz:
                bzl = bz_hop(s, h + 1)
            if h < lz:
                bzs.wait_recv()
                if h < lz - 1:
                    bzs = bz_hop(-s, h + 1)
        if h <= ly:
            wl.wait_recv()
            if h < ly:
                wl = w_hop(s, h + 1)
            w_sib(s, h)
            if h < ly:
                ws.wait_recv()
                if h < ly - 1:
                    ws = w_hop(-s, h + 1)
                w_sib(-s, h)
    bxl = bx_hop(s, 1)
    bxs = bx_hop(-s, 1) if lx > 1 else None
    t_sib(bx_piece(s, 0))

    state = dict(azl=azl, azs=azs, bxl=bxl, bxs=bxs)

    def az_step(h):
        if h > lz:
            return
        state["azl"].wait_recv()
        if h < lz:
            state["azl"] = az_hop(s, h + 1)
        t_sib(az_piece(s, h))
        if h < lz:
            state["azs"].wait_recv()
            if h < lz - 1:
                state["azs"] = az_hop(-s, h + 1)
            t_sib(az_piece(-s, h))

    def bx_step(h):
        if h > lx:
            return
        state["bxl"].wait_recv()
        if h < lx:
            state["bxl"] = bx_hop(s, h + 1)
        t_sib(bx_piece(s, h))
        if h < lx:
            state["bxs"].wait_recv()
            if h < lx - 1:
                state["bxs"] = bx_hop(-s, h + 1)
            t_sib(bx_piece(-s, h))

    az_step(1)
    az_step(2)

    for g in g_copies:
        g.wait_recv()
    g_own.wait()
    for w in sib_w:
        w.wait_recv()

    def grad_rows(i, _):
        parts = []
        for b in range(2):
            parts.append(
                jnp.concatenate([Wt[idx_ref[2 * i + b, t]] for t in range(n_mem)], axis=1)
            )
        lhs = jnp.concatenate(parts, axis=0)
        rhs = Gr[...].reshape(n_mem * TILE, width)
        r = jnp.dot(lhs, rhs, preferred_element_type=jnp.float32)
        at = row(i * 2 * BLOCK, 2 * BLOCK)
        acc[0, at, :] = r[:, :HALF]
        acc[1, at, :] = r[:, HALF:]
        return 0

    lax.fori_loop(0, blocks // 2, grad_rows, 0)

    def chunk(half, start, size):
        return (half, row(start, size), slice(None))

    def a_send(d, hops, h, bufs):
        dest = wrap(x + d * (hops - h + 1), nx)
        own_part = chunk(0, dest * xr, xr)
        if h == 1:
            src = acc.at[own_part]
        else:
            bufs[h - 2][...] += acc[own_part]
            src = bufs[h - 2]
        return remote(src, bufs[h - 1], next_x(d))

    def b_send(d, hops, h, bufs):
        dest = wrap(z + d * (hops - h + 1), nz)
        own_part = chunk(1, dest * zr, zr)
        if h == 1:
            src = acc.at[own_part]
        else:
            bufs[h - 2][...] += acc[own_part]
            src = bufs[h - 2]
        return remote(src, bufs[h - 1], next_z(d))

    ra_l, ra_s = [ra.at[i] for i in range(lx)], [ra.at[lx + i] for i in range(lx - 1)]
    rb_l, rb_s = [rb.at[i] for i in range(lz)], [rb.at[lz + i] for i in range(lz - 1)]
    al = a_send(s, lx, 1, ra_l)
    as_ = a_send(-s, lx - 1, 1, ra_s) if lx > 1 else None
    bl = b_send(s, lz, 1, rb_l)
    bs = b_send(-s, lz - 1, 1, rb_s) if lz > 1 else None
    bx_step(1)
    second_a = []
    for h in range(1, max(lx, lz) + 1):
        if h <= lz:
            bl.wait_recv()
            if h < lz:
                bl = b_send(s, lz, h + 1, rb_l)
            if h < lz:
                bs.wait_recv()
                if h < lz - 1:
                    bs = b_send(-s, lz - 1, h + 1, rb_s)
        if h <= lx:
            al.wait_recv()
            if h < lx:
                al = a_send(s, lx, h + 1, ra_l)
            if h < lx:
                as_.wait_recv()
                if h < lx - 1:
                    as_ = a_send(-s, lx - 1, h + 1, ra_s)
        if h == lx:
            mine = chunk(0, x * xr, xr)
            total = acc[mine] + ra_l[-1][...]
            if lx > 1:
                total = total + ra_s[-1][...]
            acc[mine] = total
            for k in range(1, nz):
                src = acc.at[chunk(0, x * xr + wrap(z + k, nz) * sh, sh)]
                second_a.append(remote(src, r2a.at[k - 1], next_z(k)))
        if h == 1:
            az_step(3)
    mine = chunk(1, z * zr, zr)
    total = acc[mine] + rb_l[-1][...]
    if lz > 1:
        total = total + rb_s[-1][...]
    acc[mine] = total
    second_b = []
    for k in range(1, nx):
        src = acc.at[chunk(1, z * zr + wrap(x + k, nx) * sh, sh)]
        second_b.append(remote(src, r2b.at[k - 1], next_x(k)))

    for r in second_a:
        r.wait_recv()
    mine_a = chunk(0, x * xr + z * sh, sh)
    total = acc[mine_a]
    for k in range(nz - 1):
        total = total + r2a[k]
    O[mine_a] = total.astype(jnp.bfloat16)
    out_az = [remote(O.at[mine_a], O.at[mine_a], next_z(k)) for k in range(1, nz)]
    for r in second_b:
        r.wait_recv()
    mine_b = chunk(1, z * zr + x * sh, sh)
    total = acc[mine_b]
    for k in range(nx - 1):
        total = total + r2b[k]
    O[mine_b] = total.astype(jnp.bfloat16)
    out_bx = [remote(O.at[mine_b], O.at[mine_b], next_x(k)) for k in range(1, nx)]

    bx_step(2)
    az_step(4)

    for r in out_az:
        r.wait_recv()
    piece = O.at[chunk(0, x * xr, xr)]
    out_ax = [remote(piece, piece, next_x(k)) for k in range(1, nx)]
    for r in out_bx:
        r.wait_recv()

    def ob_hop(d, h):
        p = O.at[chunk(1, wrap(z - d * (h - 1), nz) * zr, zr)]
        return remote(p, p, next_z(d))

    obl = ob_hop(s, 1)
    obs = ob_hop(-s, 1) if lz > 1 else None

    own.wait()
    for t in sib_t:
        t.wait_recv()
    GW[...] = jnp.zeros_like(GW)
    def columns(i, _):
        j, cc = i // 2, i % 2
        at = row((((j + y) % ny) * 2 + cc) * width, width)
        sel = jnp.concatenate(
            [T[j, cc, ids_ref[mem, k]] for k in range(SEL)], axis=0
        )
        V[:, at] = jnp.dot(w_ref[...], sel, preferred_element_type=jnp.float32).astype(jnp.bfloat16)
        GW[...] += lax.dot_general(
            g_ref[:, at], sel, (((1,), (1,)), ((), ())), preferred_element_type=jnp.float32
        )
        return 0

    def some(lo, hi):
        lax.fori_loop(lo, hi, columns, 0)

    part = (n_mem + lz - 1) // lz
    for h in range(1, lz + 1):
        some(min((h - 1) * part, n_mem), min(h * part, n_mem))
        obl.wait_recv()
        if h < lz:
            obl = ob_hop(s, h + 1)
        if h < lz:
            obs.wait_recv()
            if h < lz - 1:
                obs = ob_hop(-s, h + 1)
    gw_ref[...] = GW[...].astype(jnp.bfloat16)
    v_out = pltpu.make_async_copy(V, vout_ref, local.at[2])
    v_out.start()
    for r in out_ax:
        r.wait_recv()
    t_outs = [
        pltpu.make_async_copy(O.at[h], tout_ref.at[:, h * HALF:(h + 1) * HALF], local.at[3 + h])
        for h in range(2)
    ]
    for t in t_outs:
        t.start()
    for r in everything:
        r.wait_send()
    v_out.wait()
    for t in t_outs:
        t.wait()


def shards(nx, ny, nz, table, block_ids, weights, grad_out):
    rows, width = table.shape
    n_mem = 2 * ny
    blocks = rows // BLOCK
    hit = block_ids[None, :, :] == jnp.arange(blocks, dtype=jnp.int32)[:, None, None]
    at = jnp.arange(n_mem, dtype=jnp.int32)[:, None] * SEL + jnp.arange(SEL, dtype=jnp.int32)[None, :]
    idx = jnp.min(jnp.where(hit, at[None], n_mem * SEL), axis=-1)
    xr, zr, sh = rows // nx, rows // nz, rows // (nx * nz)
    n_copies = 160
    vmem = pl.BlockSpec(memory_space=pltpu.VMEM)
    smem = pl.BlockSpec(memory_space=pltpu.SMEM)
    hbm = pl.BlockSpec(memory_space=pl.ANY)
    return pl.pallas_call(
        functools.partial(kernel, nx, ny, nz, rows, width),
        out_shape=(
            jax.ShapeDtypeStruct(grad_out.shape, jnp.bfloat16),
            jax.ShapeDtypeStruct(weights.shape, jnp.bfloat16),
            jax.ShapeDtypeStruct(table.shape, jnp.bfloat16),
        ),
        in_specs=[smem, smem, hbm, vmem, vmem],
        out_specs=(hbm, vmem, hbm),
        scratch_shapes=[
            pltpu.VMEM((ny, 2, blocks, BLOCK, width), jnp.bfloat16),
            pltpu.VMEM((n_mem * SEL + 1, BLOCK, TILE), jnp.bfloat16),
            pltpu.VMEM((n_mem, TILE, width), jnp.bfloat16),
            pltpu.VMEM((2, rows, HALF), jnp.float32),
            pltpu.VMEM((nx - 1, xr, HALF), jnp.float32),
            pltpu.VMEM((nz - 1, zr, HALF), jnp.float32),
            pltpu.VMEM((nz - 1, sh, HALF), jnp.float32),
            pltpu.VMEM((nx - 1, sh, HALF), jnp.float32),
            pltpu.VMEM((2, rows, HALF), jnp.bfloat16),
            pltpu.VMEM(grad_out.shape, jnp.bfloat16),
            pltpu.VMEM(weights.shape, jnp.float32),
            pltpu.SemaphoreType.DMA((n_copies,)),
            pltpu.SemaphoreType.DMA((n_copies,)),
            pltpu.SemaphoreType.DMA((5,)),
        ],
        compiler_params=pltpu.CompilerParams(
            collective_id=0, has_side_effects=True, vmem_limit_bytes=56 * 1024 * 1024
        ),
    )(block_ids, idx, table.reshape(blocks, BLOCK, width), weights, grad_out)


def solution(mesh):
    nx = NX
    nz = mesh.shape["dp"] // nx
    ny = mesh.shape["mem"] // 2
    return jax.shard_map(
        functools.partial(shards, nx, ny, nz),
        mesh=mesh,
        in_specs=(P(None, "mem"), P("dp", None), P(("dp", "mem"), None), P(("dp", "mem"), None)),
        out_specs=(P(("dp", "mem"), None), P(("dp", "mem"), None), P(None, "mem")),
        check_vma=False,
    )
```

time: 283 us -> 141 us (0.50)
  the two profiles are of different devices: /device:TPU:8 before, /device:TPU:16 now
where the time goes in v1:
time: 141 us
  Pallas kernels  135 us (96%)
  local copies, waits for them, and re-layouts  5.35 us (4%)
    pallas_call x1, Pallas kernels, shards(): pl.pallas_call(functools.partial(kernel, nx, ny, nz, rows, width), out_sh...  135 us
    unnamed x10, local copies, waits for them, and re-layouts  5.35 us

profile of v1, /device:TPU:16, one launch (start us, length us, event | category | flops | bytes accessed | tf_op | source)
XLA Modules:
  0.0 141.2 jit_solution(1626694000922797159)
XLA Ops:
  0.6 0.0 copy-start.2
  0.7 0.7 copy-done.2
  1.3 0.6 select_reduce_fusion.idx_ref
  1.9 0.7 copy.9.ids_ref
  2.6 134.6 %shard_map.67 = (bf16[128,4096]{1,0:T(8,128)(2,1)}, bf16[128,512]{1,0:T(8,128)(2,1)}, bf16[2048,256]{1,0:T(8,128)(2,1)}) custom-call(s32[16,4]{1,0:T(8,128)} %copy.9.ids_ref, s32[16,16]{1,0:T(8,128)} %select_reduce_fusion.idx_ref, bf16[16,128,256]{2,1,0:T(8,128)(2,1)} %bitcast.1, bf16[128,512]{1,0:T(8,128)(2,1)} %w_ref.1, bf16[128,4096]{1,0:T(8,128)(2,1)} %g_ref.1), custom_call_target="tpu_custom_call" | custom-call | tf_op jit(solution)/shard_map/pallas_call | solution.py:416
  137.2 0.0 copy-start.1
  137.2 0.0 copy-start
  137.2 2.4 %copy.13 = bf16[128,4096]{1,0:T(8,128)(2,1)} copy(bf16[128,4096]{1,0:T(8,128)(2,1)} %get-tuple-element.6) | data formatting | bytes 2097152
  139.6 0.0 copy-done.1
  139.6 0.7 copy.14
  140.2 0.0 copy-done
  140.2 1.0 copy.15
  (2 shorter events, 0.0 us)
Async XLA Ops:
  0.6 0.7 copy-start.2
  137.2 2.4 %copy-start.1 = (bf16[128,512]{1,0:T(8,128)(2,1)S(1)}, bf16[128,512]{1,0:T(8,128)(2,1)}, u32[]{:S(2)}) copy-start(bf16[128,512]{1,0:T(8,128)(2,1)} %get-tuple-element.7) | copy-start | bytes 393220
  137.2 3.1 %copy-start = (bf16[2048,256]{1,0:T(8,128)(2,1)S(1)}, bf16[2048,256]{1,0:T(8,128)(2,1)}, u32[]{:S(2)}) copy-start(bf16[2048,256]{1,0:T(8,128)(2,1)} %get-tuple-element.8) | copy-start | bytes 3145732

commit v2 on v0

v2 whole, which is shorter than its diff:
```python
import functools

import jax
import jax.numpy as jnp
from jax import lax
from jax.experimental import pallas as pl
from jax.experimental.pallas import tpu as pltpu
from jax.sharding import PartitionSpec as P

MESH = pl.DeviceIdType.MESH
BLOCK = 128
SEL = 4
TILE = 128
HALF = 128
NX = 4
N_SEMS = 72


def kernel(
    nx, ny, nz, rows, width,
    ids_ref, idx_ref, table_ref, w_ref, g_ref,
    vout_ref, gw_ref, tout_ref,
    T, N, Wt, Gr, acc, rp1, rp2, rq1, rq2, O, V, GW,
    send, recv, local,
):
    dp, mem = lax.axis_index("dp"), lax.axis_index("mem")
    z, x = dp // nx, dp % nx
    y, c = mem // 2, mem % 2
    s = 1 - 2 * c
    n_mem = 2 * ny
    blocks = rows // BLOCK
    zero_slot = n_mem * SEL
    far = ny - 3
    na = 2 * far // 5
    xr, zr, sh = rows // nx, rows // nz, rows // (nx * nz)
    lx, lz, ly = nx // 2, nz // 2, ny // 2

    def dev(xx, yy, zz, cc):
        return (zz * nx + xx, yy * 2 + cc)

    sib = dev(x, y, z, 1 - c)

    def wrap(v, n):
        return (v + 4 * n) % n

    def row(start, size):
        return pl.ds(pl.multiple_of(start, size), size)

    def rows_of(ref, lead, start, size):
        if size >= BLOCK:
            return ref.at[(*lead, pl.ds(start // BLOCK, size // BLOCK))]
        return ref.at[(*lead, start // BLOCK, row(start % BLOCK, size))]

    def next_x(d):
        return dev(wrap(x + d, nx), y, z, c)

    def next_y(d):
        return dev(x, wrap(y + d, ny), z, c)

    def next_z(d):
        return dev(x, y, wrap(z + d, nz), c)

    used = [0]
    ends = []

    class Group:
        def __init__(self, out=None, into=None):
            self.k = used[0]
            used[0] += 1
            self.out, self.into = out, into
            ends.append(self)

        def start(self, src, dst, device):
            copy = pltpu.make_async_remote_copy(
                src_ref=src, dst_ref=dst, send_sem=send.at[self.k], recv_sem=recv.at[self.k],
                device_id=device, device_id_type=MESH,
            )
            copy.start()
            if self.out is None:
                self.out = src
            if self.into is None:
                self.into = dst
            return self

        def wait_recv(self):
            pltpu.make_async_copy(self.into, self.into, recv.at[self.k]).wait()

        def wait_send(self):
            pltpu.make_async_copy(self.out, self.out, send.at[self.k]).wait()

    def one(src, dst, device):
        return Group().start(src, dst, device)

    own = pltpu.make_async_copy(table_ref, T.at[0, c], local.at[0])
    own.start()
    g_own = [
        pltpu.make_async_copy(g_ref.at[:, row(mem * width + h * HALF, HALF)], Gr.at[h, mem], local.at[1 + h])
        for h in range(2)
    ]
    for g in g_own:
        g.start()
    barrier = pltpu.get_barrier_semaphore()
    peers = [(min(k // 2, ny - k // 2), (dp, (mem + k) % n_mem)) for k in range(1, n_mem)]
    peers += [(min(k, nx - k), next_x(k)) for k in range(1, nx)]
    peers += [(min(k, nz - k), next_z(k)) for k in range(1, nz)]
    peers = [p for _, p in sorted(peers, key=lambda p: -p[0])]
    for p in peers:
        pl.semaphore_signal(barrier, inc=1, device_id=p, device_id_type=MESH)
    Wt[zero_slot] = jnp.zeros((BLOCK, TILE), jnp.bfloat16)
    for k in range(SEL):
        Wt[mem * SEL + k] = w_ref[:, k * BLOCK:(k + 1) * BLOCK].astype(jnp.float32).T.astype(jnp.bfloat16)
    pl.semaphore_wait(barrier, len(peers))

    share_a, share_b = z * zr + x * sh, x * xr + z * sh
    a_planes, b_planes = slice(1, 1 + na), slice(1 + na, 1 + far)
    in_a = rows_of(T, (a_planes, c), share_a, sh)
    in_b = rows_of(T, (b_planes, c), share_b, sh)
    shares_a, shares_b = Group(in_a, in_a), Group(in_b, in_b)
    for i in sorted(range(1, 1 + far), key=lambda i: min(i + 1, ny - i - 1)):
        group, at = (shares_a, share_a) if i <= na else (shares_b, share_b)
        group.start(rows_of(table_ref, (), at, sh), rows_of(T, (i, c), at, sh), next_y(-(i + 1)))

    def w_piece(d, back):
        return Wt.at[pl.ds((wrap(y - d * back, ny) * 2 + c) * SEL, SEL)]

    def w_hop(d, h):
        p = w_piece(d, h - 1)
        return one(p, p, next_y(d))

    all_w = Wt.at[0:ny * SEL]
    sib_w = Group(all_w, all_w)

    def w_sib(d, back):
        p = w_piece(d, back)
        sib_w.start(p, p, sib)

    wl, ws = w_hop(s, 1), w_hop(-s, 1)
    w_sib(s, 0)
    sib_t = Group(T.at[:, c], T.at[:, 1 - c])
    sib_t.start(table_ref, T.at[0, c], sib)

    def t_sib(p):
        sib_t.start(p, p, sib)

    def g_send(h):
        others = Gr.at[h, 0:n_mem - 1]
        group = Group(others, others)
        for k in sorted(range(1, n_mem), key=lambda k: min(k // 2, ny - k // 2)):
            m = (mem + k) % n_mem
            group.start(g_ref.at[:, row(m * width + h * HALF, HALF)], Gr.at[h, mem], (dp, m))
        return group

    g1 = g_send(0)

    def ax_piece(back):
        return rows_of(T, (a_planes, c), z * zr + wrap(x - back, nx) * sh, sh)

    def az_piece(i, d, back):
        return rows_of(T, (i, c), wrap(z - d * back, nz) * zr, zr)

    def az_chunk(d, back):
        return rows_of(T, (a_planes, c), wrap(z - d * back, nz) * zr, zr)

    def b_piece(dx, xback, dz, zback):
        return rows_of(T, (b_planes, c), wrap(x - dx * xback, nx) * xr + wrap(z - dz * zback, nz) * sh, sh)

    def bx_chunk(d, back):
        return rows_of(T, (b_planes, c), wrap(x - d * back, nx) * xr, xr)

    def bz_hop(d, h):
        p = b_piece(s, 0, d, h - 1)
        return one(p, p, next_z(d))

    bx_short = Group(bx_chunk(-s, 0), bx_chunk(-s, 1))
    bx_last = Group(bx_chunk(s, 1), bx_chunk(s, 2))
    bx_first = {}

    def bx_start(d, back):
        p = b_piece(s, 0, d, back)
        bx_first[(d is s, back)] = one(p, p, next_x(s))
        bx_short.start(p, p, next_x(-s))

    def bx_forward(d, back):
        bx_first[(d is s, back)].wait_recv()
        p = b_piece(s, 1, d, back)
        bx_last.start(p, p, next_x(s))

    minus = -s
    shares_a.wait_recv()
    others = T.at[a_planes, c, 0, pl.ds(0, (nx - 1) * sh)] if (nx - 1) * sh <= BLOCK else None
    ax = []
    for k in range(1, nx):
        p = ax_piece(0)
        ax.append(one(p, p, next_x(k)))
    shares_b.wait_recv()
    bzl, bzs = bz_hop(s, 1), bz_hop(minus, 1) if lz > 1 else None
    bx_start(s, 0)

    azl, azs = {}, {}

    def az_step(h):
        if h > lz:
            return
        for i in range(1, 1 + na):
            if h > 0:
                azl[i].wait_recv()
            if h < lz:
                p = az_piece(i, s, h)
                azl[i] = one(p, p, next_z(s))
            if 0 < h < lz:
                azs[i].wait_recv()
            if h < lz - 1:
                p = az_piece(i, minus, h)
                azs[i] = one(p, p, next_z(minus))
        t_sib(az_chunk(s, h))
        if 0 < h < lz:
            t_sib(az_chunk(minus, h))

    def w_step(h):
        nonlocal wl, ws
        if h > ly:
            return
        wl.wait_recv()
        if h < ly:
            wl = w_hop(s, h + 1)
        w_sib(s, h)
        if h < ly:
            ws.wait_recv()
            if h < ly - 1:
                ws = w_hop(minus, h + 1)
            w_sib(minus, h)

    def bz_step(h):
        nonlocal bzl, bzs
        if h > lz:
            return
        bzl.wait_recv()
        if h < lz:
            bzl = bz_hop(s, h + 1)
        bx_start(s, h)
        if h < lz:
            bzs.wait_recv()
            if h < lz - 1:
                bzs = bz_hop(minus, h + 1)
            bx_start(minus, h)

    def bx_step(h):
        if h > lz:
            return
        bx_forward(s, h)
        if 0 < h < lz:
            bx_forward(minus, h)

    w_step(1)
    bz_step(1)
    for r in ax:
        r.wait_recv()
    az_step(0)
    w_step(2)
    bz_step(2)
    bx_step(0)
    w_step(3)
    g2 = g_send(1)
    az_step(1)
    bz_step(3)
    bx_step(1)
    w_step(4)
    bz_step(4)
    t_sib(bx_chunk(s, 0))
    az_step(2)
    bx_step(2)

    def grad(h):
        def grad_rows(i, _):
            parts = []
            for b in range(2):
                parts.append(
                    jnp.concatenate([Wt[idx_ref[2 * i + b, t]] for t in range(n_mem)], axis=1)
                )
            lhs = jnp.concatenate(parts, axis=0)
            rhs = Gr[h].reshape(n_mem * TILE, HALF)
            r = jnp.dot(lhs, rhs, preferred_element_type=jnp.float32)
            acc[h, row(i * 2 * BLOCK, 2 * BLOCK), :] = r
            return 0

        lax.fori_loop(0, blocks // 2, grad_rows, 0)

    top = rows // 2
    px, pz = top // nx, top // (nx * nz)
    qz, qx = top // nz, top // (nx * nz)

    def reduction(h):
        def at(ref, start, size):
            return ref.at[h, row(start, size), :]

        def bytes_of(ref, size):
            return ref.at[h, 0:size, :]

        def p1():
            group = Group(rp1.at[h], rp1.at[h])
            for k in range(1, nx):
                group.start(at(acc, wrap(x + k, nx) * px, px), rp1.at[h, k - 1], next_x(k))
            return group

        def q1():
            group = Group(rq1.at[h], rq1.at[h])
            for k in range(1, nz):
                group.start(at(acc, top + wrap(z + k, nz) * qz, qz), rq1.at[h, k - 1], next_z(k))
            return group

        def p2():
            mine = row(x * px, px)
            total = acc[h, mine, :]
            for k in range(nx - 1):
                total = total + rp1[h, k]
            acc[h, mine, :] = total
            group = Group(rp2.at[h], rp2.at[h])
            for k in range(1, nz):
                group.start(at(acc, x * px + wrap(z + k, nz) * pz, pz), rp2.at[h, k - 1], next_z(k))
            return group

        def q2():
            mine = row(top + z * qz, qz)
            total = acc[h, mine, :]
            for k in range(nz - 1):
                total = total + rq1[h, k]
            acc[h, mine, :] = total
            group = Group(rq2.at[h], rq2.at[h])
            for k in range(1, nx):
                group.start(at(acc, top + z * qz + wrap(x + k, nx) * qx, qx), rq2.at[h, k - 1], next_x(k))
            return group

        def p3():
            mine = row(x * px + z * pz, pz)
            total = acc[h, mine, :]
            for k in range(nz - 1):
                total = total + rp2[h, k]
            O[h, mine, :] = total.astype(jnp.bfloat16)
            group = Group(bytes_of(O, (nz - 1) * pz), bytes_of(O, (nz - 1) * pz))
            piece = at(O, x * px + z * pz, pz)
            for k in range(1, nz):
                group.start(piece, piece, next_z(k))
            return group

        def q3():
            mine = row(top + z * qz + x * qx, qx)
            total = acc[h, mine, :]
            for k in range(nx - 1):
                total = total + rq2[h, k]
            O[h, mine, :] = total.astype(jnp.bfloat16)
            group = Group(bytes_of(O, (nx - 1) * qx), bytes_of(O, (nx - 1) * qx))
            piece = at(O, top + z * qz + x * qx, qx)
            for k in range(1, nx):
                group.start(piece, piece, next_x(k))
            return group

        def p4():
            group = Group(bytes_of(O, (nx - 1) * px), bytes_of(O, (nx - 1) * px))
            piece = at(O, x * px, px)
            for k in range(1, nx):
                group.start(piece, piece, next_x(k))
            return group

        def q4():
            group = Group(bytes_of(O, (nz - 1) * qz), bytes_of(O, (nz - 1) * qz))
            piece = at(O, top + z * qz, qz)
            for k in range(1, nz):
                group.start(piece, piece, next_z(k))
            return group

        p, q = p1(), q1()
        yield
        p.wait_recv()
        p = p2()
        q.wait_recv()
        q = q2()
        yield
        q.wait_recv()
        q = q3()
        p.wait_recv()
        p = p3()
        yield
        q.wait_recv()
        q = q4()
        p.wait_recv()
        p = p4()
        yield
        p.wait_recv()
        q.wait_recv()
        yield

    def columns(table, i, cc, plane):
        at = row((plane * 2 + cc) * width, width)
        sel = jnp.concatenate([table[i, cc, ids_ref[mem, k]] for k in range(SEL)], axis=0)
        V[:, at] = jnp.dot(w_ref[...], sel, preferred_element_type=jnp.float32).astype(jnp.bfloat16)
        GW[...] += lax.dot_general(
            g_ref[:, at], sel, (((1,), (1,)), ((), ())), preferred_element_type=jnp.float32
        )

    def own_column(k, _):
        i, cc = k // 2, k % 2
        columns(T, i, cc, (y + jnp.where(i == 0, 0, i + 1)) % ny)
        return 0

    def near_column(k, _):
        i, cc = k // 2, k % 2
        columns(N, i, cc, (y + jnp.where(i == 0, 1, ny - 1)) % ny)
        return 0

    g1.wait_recv()
    sib_w.wait_recv()
    for g in g_own:
        g.wait()
    grad(0)
    first = reduction(0)
    next(first)
    az_step(3)
    bx_step(3)
    bx_step(4)
    next(first)
    g2.wait_recv()
    grad(1)
    second = reduction(1)
    next(second)
    near = [
        one(table_ref, N.at[0, c], next_y(-1)),
        one(table_ref, N.at[1, c], next_y(1)),
    ]
    next(first)
    az_step(4)
    bx_short.wait_recv()
    t_sib(bx_chunk(minus, 1))
    next(first)
    bx_last.wait_recv()
    t_sib(bx_chunk(s, 2))
    for k in (1,):
        t_sib(bx_chunk(s, k))
    next(second)
    next(first)
    t_out = [
        pltpu.make_async_copy(O.at[h], tout_ref.at[:, h * HALF:(h + 1) * HALF], local.at[3 + h])
        for h in range(2)
    ]
    t_out[0].start()
    own.wait()
    sib_t.wait_recv()
    GW[...] = jnp.zeros_like(GW)
    lax.fori_loop(0, 2 * (1 + far), own_column, 0)
    next(second)
    sib_n = Group(N.at[:, c], N.at[:, 1 - c])
    for i in range(2):
        near[i].wait_recv()
        sib_n.start(N.at[i, c], N.at[i, c], sib)
    next(second)
    sib_n.wait_recv()
    lax.fori_loop(0, 4, near_column, 0)
    v_out = pltpu.make_async_copy(V, vout_ref, local.at[5])
    v_out.start()
    gw_ref[...] = GW[...].astype(jnp.bfloat16)
    next(second)
    t_out[1].start()
    for group in ends:
        group.wait_send()
    v_out.wait()
    for t in t_out:
        t.wait()
    assert used[0] <= N_SEMS, used[0]


def shards(nx, ny, nz, table, block_ids, weights, grad_out):
    rows, width = table.shape
    n_mem = 2 * ny
    blocks = rows // BLOCK
    hit = block_ids[None, :, :] == jnp.arange(blocks, dtype=jnp.int32)[:, None, None]
    at = jnp.arange(n_mem, dtype=jnp.int32)[:, None] * SEL + jnp.arange(SEL, dtype=jnp.int32)[None, :]
    idx = jnp.min(jnp.where(hit, at[None], n_mem * SEL), axis=-1)
    top = rows // 2
    vmem = pl.BlockSpec(memory_space=pltpu.VMEM)
    smem = pl.BlockSpec(memory_space=pltpu.SMEM)
    hbm = pl.BlockSpec(memory_space=pl.ANY)
    return pl.pallas_call(
        functools.partial(kernel, nx, ny, nz, rows, width),
        out_shape=(
            jax.ShapeDtypeStruct(grad_out.shape, jnp.bfloat16),
            jax.ShapeDtypeStruct(weights.shape, jnp.bfloat16),
            jax.ShapeDtypeStruct(table.shape, jnp.bfloat16),
        ),
        in_specs=[smem, smem, hbm, vmem, vmem],
        out_specs=(hbm, vmem, hbm),
        scratch_shapes=[
            pltpu.VMEM((ny - 2, 2, blocks, BLOCK, width), jnp.bfloat16),
            pltpu.VMEM((2, 2, blocks, BLOCK, width), jnp.bfloat16),
            pltpu.VMEM((n_mem * SEL + 1, BLOCK, TILE), jnp.bfloat16),
            pltpu.VMEM((2, n_mem, TILE, HALF), jnp.bfloat16),
            pltpu.VMEM((2, rows, HALF), jnp.float32),
            pltpu.VMEM((2, nx - 1, top // nx, HALF), jnp.float32),
            pltpu.VMEM((2, nz - 1, top // (nx * nz), HALF), jnp.float32),
            pltpu.VMEM((2, nz - 1, top // nz, HALF), jnp.float32),
            pltpu.VMEM((2, nx - 1, top // (nx * nz), HALF), jnp.float32),
            pltpu.VMEM((2, rows, HALF), jnp.bfloat16),
            pltpu.VMEM(grad_out.shape, jnp.bfloat16),
            pltpu.VMEM(weights.shape, jnp.float32),
            pltpu.SemaphoreType.DMA((N_SEMS,)),
            pltpu.SemaphoreType.DMA((N_SEMS,)),
            pltpu.SemaphoreType.DMA((6,)),
        ],
        compiler_params=pltpu.CompilerParams(
            collective_id=0, has_side_effects=True, vmem_limit_bytes=56 * 1024 * 1024
        ),
    )(block_ids, idx, table.reshape(blocks, BLOCK, width), weights, grad_out)


def solution(mesh):
    nx = NX
    nz = mesh.shape["dp"] // nx
    ny = mesh.shape["mem"] // 2
    return jax.shard_map(
        functools.partial(shards, nx, ny, nz),
        mesh=mesh,
        in_specs=(P(None, "mem"), P("dp", None), P(("dp", "mem"), None), P(("dp", "mem"), None)),
        out_specs=(P(("dp", "mem"), None), P(("dp", "mem"), None), P(None, "mem")),
        check_vma=False,
    )
```

time: 283 us -> 123 us (0.43)
  the two profiles are of different devices: /device:TPU:8 before, /device:TPU:1 now
where the time goes in v2:
time: 123 us
  Pallas kernels  116 us (94%)
  local copies, waits for them, and re-layouts  5.35 us (4%)
    pallas_call x1, Pallas kernels, shards(): pl.pallas_call(functools.partial(kernel, nx, ny, nz, rows, width), out_sh...  116 us
    unnamed x10, local copies, waits for them, and re-layouts  5.35 us

profile of v2, /device:TPU:1, one launch (start us, length us, event | category | flops | bytes accessed | tf_op | source)
XLA Modules:
  0.0 122.7 jit_solution(4005424807809001663)
XLA Ops:
  0.6 0.0 copy-start.2
  0.7 0.7 copy-done.2
  1.3 0.6 select_reduce_fusion.idx_ref
  1.9 0.7 copy.9.ids_ref
  2.6 116.0 %shard_map.67 = (bf16[128,4096]{1,0:T(8,128)(2,1)}, bf16[128,512]{1,0:T(8,128)(2,1)}, bf16[2048,256]{1,0:T(8,128)(2,1)}) custom-call(s32[16,4]{1,0:T(8,128)} %copy.9.ids_ref, s32[16,16]{1,0:T(8,128)} %select_reduce_fusion.idx_ref, bf16[16,128,256]{2,1,0:T(8,128)(2,1)} %bitcast.1, bf16[128,512]{1,0:T(8,128)(2,1)} %w_ref.1, bf16[128,4096]{1,0:T(8,128)(2,1)} %g_ref.1), custom_call_target="tpu_custom_call" | custom-call | tf_op jit(solution)/shard_map/pallas_call | solution.py:481
  118.6 0.0 copy-start.1
  118.6 0.0 copy-start
  118.6 2.4 %copy.13 = bf16[128,4096]{1,0:T(8,128)(2,1)} copy(bf16[128,4096]{1,0:T(8,128)(2,1)} %get-tuple-element.6) | data formatting | bytes 2097152
  121.0 0.0 copy-done.1
  121.0 0.7 copy.14
  121.7 0.0 copy-done
  121.7 1.0 copy.15
  (2 shorter events, 0.0 us)
Async XLA Ops:
  0.6 0.7 copy-start.2
  118.6 2.4 %copy-start.1 = (bf16[128,512]{1,0:T(8,128)(2,1)S(1)}, bf16[128,512]{1,0:T(8,128)(2,1)}, u32[]{:S(2)}) copy-start(bf16[128,512]{1,0:T(8,128)(2,1)} %get-tuple-element.7) | copy-start | bytes 393220
  118.6 3.1 %copy-start = (bf16[2048,256]{1,0:T(8,128)(2,1)S(1)}, bf16[2048,256]{1,0:T(8,128)(2,1)}, u32[]{:S(2)}) copy-start(bf16[2048,256]{1,0:T(8,128)(2,1)} %get-tuple-element.8) | copy-start | bytes 3145732

commit v3 on v2

--- a/solution.py
+++ b/solution.py
@@ -18,9 +18,9 @@
 
 def kernel(
     nx, ny, nz, rows, width,
-    ids_ref, idx_ref, table_ref, w_ref, g_ref,
+    ids_ref, ids_vmem, table_ref, w_ref, g_ref,
     vout_ref, gw_ref, tout_ref,
-    T, N, Wt, Gr, acc, rp1, rp2, rq1, rq2, O, V, GW,
+    T, N, idx_vmem, idx_ref, Wt, Gr, acc, rp1, rp2, rq1, rq2, O, V, GW,
     send, recv, local,
 ):
     dp, mem = lax.axis_index("dp"), lax.axis_index("mem")
@@ -106,6 +106,14 @@
     peers = [p for _, p in sorted(peers, key=lambda p: -p[0])]
     for p in peers:
         pl.semaphore_signal(barrier, inc=1, device_id=p, device_id_type=MESH)
+    tile_at = lax.broadcasted_iota(jnp.int32, (blocks, n_mem), 1) * SEL
+    block_at = lax.broadcasted_iota(jnp.int32, (blocks, n_mem), 0)
+    found = jnp.full((blocks, n_mem), zero_slot, jnp.int32)
+    for k in range(SEL):
+        found = jnp.where(ids_vmem[k:k + 1, :] == block_at, tile_at + k, found)
+    idx_vmem[...] = found
+    idx_copy = pltpu.make_async_copy(idx_vmem, idx_ref, local.at[6])
+    idx_copy.start()
     Wt[zero_slot] = jnp.zeros((BLOCK, TILE), jnp.bfloat16)
     for k in range(SEL):
         Wt[mem * SEL + k] = w_ref[:, k * BLOCK:(k + 1) * BLOCK].astype(jnp.float32).T.astype(jnp.bfloat16)
@@ -142,15 +150,15 @@
     def t_sib(p):
         sib_t.start(p, p, sib)
 
-    def g_send(h):
-        others = Gr.at[h, 0:n_mem - 1]
-        group = Group(others, others)
-        for k in sorted(range(1, n_mem), key=lambda k: min(k // 2, ny - k // 2)):
+    g_order = sorted(range(1, n_mem), key=lambda k: -min(k // 2, ny - k // 2))
+    g_halves = [Group(Gr.at[h, 0:n_mem - 1], Gr.at[h, 0:n_mem - 1]) for h in range(2)]
+
+    def g_send(h, lo, hi):
+        for k in g_order[lo:hi]:
             m = (mem + k) % n_mem
-            group.start(g_ref.at[:, row(m * width + h * HALF, HALF)], Gr.at[h, mem], (dp, m))
-        return group
-
-    g1 = g_send(0)
+            g_halves[h].start(g_ref.at[:, row(m * width + h * HALF, HALF)], Gr.at[h, mem], (dp, m))
+
+    g1, g2 = g_halves
 
     def ax_piece(back):
         return rows_of(T, (a_planes, c), z * zr + wrap(x - back, nx) * sh, sh)
@@ -186,16 +194,7 @@
         bx_last.start(p, p, next_x(s))
 
     minus = -s
-    shares_a.wait_recv()
-    others = T.at[a_planes, c, 0, pl.ds(0, (nx - 1) * sh)] if (nx - 1) * sh <= BLOCK else None
-    ax = []
-    for k in range(1, nx):
-        p = ax_piece(0)
-        ax.append(one(p, p, next_x(k)))
-    shares_b.wait_recv()
-    bzl, bzs = bz_hop(s, 1), bz_hop(minus, 1) if lz > 1 else None
-    bx_start(s, 0)
-
+    bzl = bzs = None
     azl, azs = {}, {}
 
     def az_step(h):
@@ -251,25 +250,6 @@
         if 0 < h < lz:
             bx_forward(minus, h)
 
-    w_step(1)
-    bz_step(1)
-    for r in ax:
-        r.wait_recv()
-    az_step(0)
-    w_step(2)
-    bz_step(2)
-    bx_step(0)
-    w_step(3)
-    g2 = g_send(1)
-    az_step(1)
-    bz_step(3)
-    bx_step(1)
-    w_step(4)
-    bz_step(4)
-    t_sib(bx_chunk(s, 0))
-    az_step(2)
-    bx_step(2)
-
     def grad(h):
         def grad_rows(i, _):
             parts = []
@@ -285,9 +265,9 @@
 
         lax.fori_loop(0, blocks // 2, grad_rows, 0)
 
-    top = rows // 2
+    top = 3 * rows // 4
     px, pz = top // nx, top // (nx * nz)
-    qz, qx = top // nz, top // (nx * nz)
+    qz, qx = (rows - top) // nz, (rows - top) // (nx * nz)
 
     def reduction(h):
         def at(ref, start, size):
@@ -391,7 +371,7 @@
 
     def columns(table, i, cc, plane):
         at = row((plane * 2 + cc) * width, width)
-        sel = jnp.concatenate([table[i, cc, ids_ref[mem, k]] for k in range(SEL)], axis=0)
+        sel = jnp.concatenate([table[i, cc, ids_ref[k, mem]] for k in range(SEL)], axis=0)
         V[:, at] = jnp.dot(w_ref[...], sel, preferred_element_type=jnp.float32).astype(jnp.bfloat16)
         GW[...] += lax.dot_general(
             g_ref[:, at], sel, (((1,), (1,)), ((), ())), preferred_element_type=jnp.float32
@@ -407,34 +387,68 @@
         columns(N, i, cc, (y + jnp.where(i == 0, 1, ny - 1)) % ny)
         return 0
 
+    def near_start():
+        return [
+            one(table_ref, N.at[0, c], next_y(-1)),
+            one(table_ref, N.at[1, c], next_y(1)),
+        ]
+
+    w_step(1)
+    g_send(0, 0, 4)
+    shares_a.wait_recv()
+    ax = []
+    for k in range(1, nx):
+        p = ax_piece(0)
+        ax.append(one(p, p, next_x(k)))
+    shares_b.wait_recv()
+    bzl, bzs = bz_hop(s, 1), bz_hop(minus, 1) if lz > 1 else None
+    bx_start(s, 0)
+
+    w_step(2)
+    g_send(0, 4, 8)
+    bz_step(1)
+    for r in ax:
+        r.wait_recv()
+    az_step(0)
+    w_step(3)
+    g_send(0, 8, n_mem)
+    bz_step(2)
+    bx_step(0)
+    w_step(4)
+    g_send(1, 0, n_mem)
+    az_step(1)
+    bz_step(3)
+    bx_step(1)
     g1.wait_recv()
     sib_w.wait_recv()
     for g in g_own:
         g.wait()
+    idx_copy.wait()
     grad(0)
     first = reduction(0)
     next(first)
-    az_step(3)
+    near = near_start()
+    bz_step(4)
+    t_sib(bx_chunk(s, 0))
+    az_step(2)
+    bx_step(2)
+    next(first)
     bx_step(3)
-    bx_step(4)
-    next(first)
     g2.wait_recv()
     grad(1)
     second = reduction(1)
     next(second)
-    near = [
-        one(table_ref, N.at[0, c], next_y(-1)),
-        one(table_ref, N.at[1, c], next_y(1)),
-    ]
+    next(first)
+    az_step(3)
+    bx_step(4)
+    t_sib(bx_chunk(s, 1))
+    next(second)
     next(first)
     az_step(4)
     bx_short.wait_recv()
     t_sib(bx_chunk(minus, 1))
-    next(first)
     bx_last.wait_recv()
     t_sib(bx_chunk(s, 2))
-    for k in (1,):
-        t_sib(bx_chunk(s, k))
     next(second)
     next(first)
     t_out = [
@@ -451,7 +465,6 @@
     for i in range(2):
         near[i].wait_recv()
         sib_n.start(N.at[i, c], N.at[i, c], sib)
-    next(second)
     sib_n.wait_recv()
     lax.fori_loop(0, 4, near_column, 0)
     v_out = pltpu.make_async_copy(V, vout_ref, local.at[5])
@@ -471,10 +484,7 @@
     rows, width = table.shape
     n_mem = 2 * ny
     blocks = rows // BLOCK
-    hit = block_ids[None, :, :] == jnp.arange(blocks, dtype=jnp.int32)[:, None, None]
-    at = jnp.arange(n_mem, dtype=jnp.int32)[:, None] * SEL + jnp.arange(SEL, dtype=jnp.int32)[None, :]
-    idx = jnp.min(jnp.where(hit, at[None], n_mem * SEL), axis=-1)
-    top = rows // 2
+    top = 3 * rows // 4
     vmem = pl.BlockSpec(memory_space=pltpu.VMEM)
     smem = pl.BlockSpec(memory_space=pltpu.SMEM)
     hbm = pl.BlockSpec(memory_space=pl.ANY)
@@ -485,29 +495,31 @@
             jax.ShapeDtypeStruct(weights.shape, jnp.bfloat16),
             jax.ShapeDtypeStruct(table.shape, jnp.bfloat16),
         ),
-        in_specs=[smem, smem, hbm, vmem, vmem],
+        in_specs=[smem, vmem, hbm, vmem, vmem],
         out_specs=(hbm, vmem, hbm),
         scratch_shapes=[
             pltpu.VMEM((ny - 2, 2, blocks, BLOCK, width), jnp.bfloat16),
             pltpu.VMEM((2, 2, blocks, BLOCK, width), jnp.bfloat16),
+            pltpu.VMEM((blocks, n_mem), jnp.int32),
+            pltpu.SMEM((blocks, n_mem), jnp.int32),
             pltpu.VMEM((n_mem * SEL + 1, BLOCK, TILE), jnp.bfloat16),
             pltpu.VMEM((2, n_mem, TILE, HALF), jnp.bfloat16),
             pltpu.VMEM((2, rows, HALF), jnp.float32),
             pltpu.VMEM((2, nx - 1, top // nx, HALF), jnp.float32),
             pltpu.VMEM((2, nz - 1, top // (nx * nz), HALF), jnp.float32),
-            pltpu.VMEM((2, nz - 1, top // nz, HALF), jnp.float32),
-            pltpu.VMEM((2, nx - 1, top // (nx * nz), HALF), jnp.float32),
+            pltpu.VMEM((2, nz - 1, (rows - top) // nz, HALF), jnp.float32),
+            pltpu.VMEM((2, nx - 1, (rows - top) // (nx * nz), HALF), jnp.float32),
             pltpu.VMEM((2, rows, HALF), jnp.bfloat16),
             pltpu.VMEM(grad_out.shape, jnp.bfloat16),
             pltpu.VMEM(weights.shape, jnp.float32),
             pltpu.SemaphoreType.DMA((N_SEMS,)),
             pltpu.SemaphoreType.DMA((N_SEMS,)),
-            pltpu.SemaphoreType.DMA((6,)),
+            pltpu.SemaphoreType.DMA((7,)),
         ],
         compiler_params=pltpu.CompilerParams(
             collective_id=0, has_side_effects=True, vmem_limit_bytes=56 * 1024 * 1024
         ),
-    )(block_ids, idx, table.reshape(blocks, BLOCK, width), weights, grad_out)
+    )(block_ids.T, block_ids.T, table.reshape(blocks, BLOCK, width), weights, grad_out)
 
 
 def solution(mesh):

time: 123 us -> 107 us (0.87)
  Pallas kernels: 116 us -> 102 us
  local copies, waits for them, and re-layouts: 5.35 us -> 4.02 us
    pallas_call x1, Pallas kernels: 116 us -> 102 us  [shards(): pl.pallas_call(functools.partial(kernel, nx, ny, nz, rows, width), out_sh...]
    unnamed x10 -> x7, local copies, waits for them, and re-layouts: 5.35 us -> 4.02 us
where the time goes in v3:
time: 107 us
  Pallas kernels  102 us (95%)
  local copies, waits for them, and re-layouts  4.02 us (4%)
    pallas_call x1, Pallas kernels, shards(): pl.pallas_call(functools.partial(kernel, nx, ny, nz, rows, width), out_sh...  102 us
    unnamed x7, local copies, waits for them, and re-layouts  4.02 us

profile of v3, /device:TPU:1, one launch (start us, length us, event | category | flops | bytes accessed | tf_op | source)
XLA Modules:
  0.0 107.1 jit_solution(647537117003503287)
XLA Ops:
  0.6 102.5 %shard_map.67 = (bf16[128,4096]{1,0:T(8,128)(2,1)}, bf16[128,512]{1,0:T(8,128)(2,1)}, bf16[2048,256]{1,0:T(8,128)(2,1)}) custom-call(s32[4,16]{1,0:T(4,128)} %bitcast.3, s32[4,16]{1,0:T(4,128)} %bitcast.4, bf16[16,128,256]{2,1,0:T(8,128)(2,1)} %bitcast.2, bf16[128,512]{1,0:T(8,128)(2,1)} %w_ref.1, bf16[128,4096]{1,0:T(8,128)(2,1)} %g_ref.1), custom_call_target="tpu_custom_call" | custom-call | tf_op jit(solution)/shard_map/pallas_call | solution.py:491
  103.1 0.0 copy-start.1
  103.1 0.0 copy-start
  103.1 2.4 %copy.10 = bf16[128,4096]{1,0:T(8,128)(2,1)} copy(bf16[128,4096]{1,0:T(8,128)(2,1)} %get-tuple-element.6) | data formatting | bytes 2097152
  105.5 0.0 copy-done.1
  105.5 0.7 copy.11
  106.2 0.0 copy-done
  106.2 1.0 copy.12
Async XLA Ops:
  103.1 2.4 %copy-start.1 = (bf16[128,512]{1,0:T(8,128)(2,1)S(1)}, bf16[128,512]{1,0:T(8,128)(2,1)}, u32[]{:S(2)}) copy-start(bf16[128,512]{1,0:T(8,128)(2,1)} %get-tuple-element.7) | copy-start | bytes 393220
  103.1 3.1 %copy-start = (bf16[2048,256]{1,0:T(8,128)(2,1)S(1)}, bf16[2048,256]{1,0:T(8,128)(2,1)}, u32[]{:S(2)}) copy-start(bf16[2048,256]{1,0:T(8,128)(2,1)} %get-tuple-element.8) | copy-start | bytes 3145732

commit v4 on v3

--- a/solution.py
+++ b/solution.py
@@ -433,18 +433,18 @@
     az_step(2)
     bx_step(2)
     next(first)
+    az_step(3)
     bx_step(3)
     g2.wait_recv()
     grad(1)
     second = reduction(1)
     next(second)
-    next(first)
-    az_step(3)
     bx_step(4)
     t_sib(bx_chunk(s, 1))
+    next(first)
+    az_step(4)
     next(second)
     next(first)
-    az_step(4)
     bx_short.wait_recv()
     t_sib(bx_chunk(minus, 1))
     bx_last.wait_recv()

time: 107 us -> 111 us (1.037)
  Pallas kernels: 102 us -> 106 us
    pallas_call x1, Pallas kernels: 102 us -> 106 us  [shards(): pl.pallas_call(functools.partial(kernel, nx, ny, nz, rows, width), out_sh...]
where the time goes in v4:
time: 111 us
  Pallas kernels  106 us (95%)
  local copies, waits for them, and re-layouts  4.02 us (4%)
    pallas_call x1, Pallas kernels, shards(): pl.pallas_call(functools.partial(kernel, nx, ny, nz, rows, width), out_sh...  106 us
    unnamed x7, local copies, waits for them, and re-layouts  4.02 us

profile of v4, /device:TPU:1, one launch (start us, length us, event | category | flops | bytes accessed | tf_op | source)
XLA Modules:
  0.0 111.1 jit_solution(10220395532304414485)
XLA Ops:
  0.6 106.4 %shard_map.67 = (bf16[128,4096]{1,0:T(8,128)(2,1)}, bf16[128,512]{1,0:T(8,128)(2,1)}, bf16[2048,256]{1,0:T(8,128)(2,1)}) custom-call(s32[4,16]{1,0:T(4,128)} %bitcast.3, s32[4,16]{1,0:T(4,128)} %bitcast.4, bf16[16,128,256]{2,1,0:T(8,128)(2,1)} %bitcast.2, bf16[128,512]{1,0:T(8,128)(2,1)} %w_ref.1, bf16[128,4096]{1,0:T(8,128)(2,1)} %g_ref.1), custom_call_target="tpu_custom_call" | custom-call | tf_op jit(solution)/shard_map/pallas_call | solution.py:491
  107.1 0.0 copy-start.1
  107.1 0.0 copy-start
  107.1 2.4 %copy.10 = bf16[128,4096]{1,0:T(8,128)(2,1)} copy(bf16[128,4096]{1,0:T(8,128)(2,1)} %get-tuple-element.6) | data formatting | bytes 2097152
  109.5 0.0 copy-done.1
  109.5 0.7 copy.11
  110.1 0.0 copy-done
  110.1 1.0 copy.12
Async XLA Ops:
  107.1 2.4 %copy-start.1 = (bf16[128,512]{1,0:T(8,128)(2,1)S(1)}, bf16[128,512]{1,0:T(8,128)(2,1)}, u32[]{:S(2)}) copy-start(bf16[128,512]{1,0:T(8,128)(2,1)} %get-tuple-element.7) | copy-start | bytes 393220
  107.1 3.1 %copy-start = (bf16[2048,256]{1,0:T(8,128)(2,1)S(1)}, bf16[2048,256]{1,0:T(8,128)(2,1)}, u32[]{:S(2)}) copy-start(bf16[2048,256]{1,0:T(8,128)(2,1)} %get-tuple-element.8) | copy-start | bytes 3145732
